TPU v7x, 512 devices: a whole 4x4x16 slice. The times are simulated.
512 devices in a mesh: gx: 32 (over y, z_hi, x), gy: 16 (over z_lo, core).
Axes of the slice: x: 4, y: 4, z: 16 (z_hi: 2, z_lo: 8; z = z_hi * 8 + z_lo), core: 2. Of those that a mesh axis runs over, the one named last changes fastest.
Arguments:
- e_field: float32 [3, 256, 256, 128], P(None, 'gx', 'gy'), may hold values from -30 to 30
- h_field: float32 [3, 256, 256, 128], P(None, 'gx', 'gy'), may hold values from -30 to 30
- material: int32 [256, 256, 64], P('gx', 'gy'), may hold values from 0 to 3
- permittivity: float32 [4], replicated, may hold values from 1 to 12
- frequencies: float32 [4], replicated, may hold values from 0.6 to 2.4
Outputs:
- e_out: float32 [3, 256, 256, 128], P(None, 'gx', 'gy')
- h_out: float32 [3, 256, 256, 128], P(None, 'gx', 'gy')
- gram: float32 [8, 8], replicated
All inputs are finite; a program needn't handle non-finite values.
Results may differ from a plain program's by a relative error of at most 0.000096.
Values sent between devices are 32-bit elements; how exact they have to be, the bound alone decides.
No kernel may reach another device: no remote copies, remote signals or barrier semaphores. Data moves between devices by JAX's collectives and lax.ppermute only.
A program may use at most 64 MiB of HBM per device.

v0:
```python
import jax
import jax.numpy as jnp
from jax import lax
from jax.sharding import PartitionSpec as P

NZ = 64
SOURCES = 2
FILTERS = 4
MATERIALS = 4
ITERS = 4
TIME_STEP = 0.5


def from_behind(value, axis, steps):
    count = lax.axis_size(axis)
    pairs = [(source, (source + steps) % count) for source in range(count)]
    return lax.ppermute(value, axis, pairs)


def forward_z(field):
    pad = jnp.zeros(field.shape[:-1] + (SOURCES,), field.dtype)
    return jnp.concatenate([field[..., SOURCES:], pad], axis=-1) - field


def backward_z(field):
    pad = jnp.zeros(field.shape[:-1] + (SOURCES,), field.dtype)
    return field - jnp.concatenate([pad, field[..., :-SOURCES]], axis=-1)


def next_values(e_field):
    plane_x = from_behind(e_field[1:3, :1], "gx", -1)
    plane_y = from_behind(jnp.stack([e_field[0][:, :1], e_field[2][:, :1]]), "gy", -1)
    ey_next_x = jnp.concatenate([e_field[1, 1:], plane_x[0]], axis=0)
    ez_next_x = jnp.concatenate([e_field[2, 1:], plane_x[1]], axis=0)
    ex_next_y = jnp.concatenate([e_field[0][:, 1:], plane_y[0]], axis=1)
    ez_next_y = jnp.concatenate([e_field[2][:, 1:], plane_y[1]], axis=1)
    return (ey_next_x, ez_next_x, ex_next_y, ez_next_y)


def prev_values(h_field):
    plane_x = from_behind(h_field[1:3, -1:], "gx", 1)
    plane_y = from_behind(jnp.stack([h_field[0][:, -1:], h_field[2][:, -1:]]), "gy", 1)
    hy_prev_x = jnp.concatenate([plane_x[0], h_field[1, :-1]], axis=0)
    hz_prev_x = jnp.concatenate([plane_x[1], h_field[2, :-1]], axis=0)
    hx_prev_y = jnp.concatenate([plane_y[0], h_field[0][:, :-1]], axis=1)
    hz_prev_y = jnp.concatenate([plane_y[1], h_field[2][:, :-1]], axis=1)
    return (hy_prev_x, hz_prev_x, hx_prev_y, hz_prev_y)


def advance(e_field, h_field, scaled, next_fn, prev_fn):
    e_x, e_y, e_z = (e_field[0], e_field[1], e_field[2])
    ey_next_x, ez_next_x, ex_next_y, ez_next_y = next_fn(e_field)
    curl_x = ez_next_y - e_z - forward_z(e_y)
    curl_y = forward_z(e_x) - (ez_next_x - e_z)
    curl_z = ey_next_x - e_y - (ex_next_y - e_x)
    h_field = h_field - TIME_STEP * jnp.stack([curl_x, curl_y, curl_z])
    h_x, h_y, h_z = (h_field[0], h_field[1], h_field[2])
    hy_prev_x, hz_prev_x, hx_prev_y, hz_prev_y = prev_fn(h_field)
    curl_x = h_z - hz_prev_y - backward_z(h_y)
    curl_y = backward_z(h_x) - (h_z - hz_prev_x)
    curl_z = h_y - hy_prev_x - (h_x - hx_prev_y)
    e_field = jnp.stack([e_x + scaled * curl_x, e_y + scaled * curl_y, e_z + scaled * curl_z])
    return (e_field, h_field)


def body(e_field, h_field, material, permittivity, frequencies):
    onehot = (material[..., None] == jnp.arange(MATERIALS, dtype=jnp.int32)).astype(jnp.float32)
    permit_cell = jnp.sum(onehot * permittivity, axis=-1)
    permit = jnp.repeat(permit_cell, SOURCES, axis=-1)
    scaled = TIME_STEP / permit
    filtered = jnp.zeros((FILTERS,) + e_field.shape, jnp.float32)
    for step in range(ITERS):
        e_field, h_field = advance(e_field, h_field, scaled, next_values, prev_values)
        weights = jnp.cos(frequencies * ((step + 1) * TIME_STEP))
        filtered = filtered + weights[:, None, None, None, None] * e_field[None]
    count = filtered[0].size // SOURCES
    weighted = (filtered * permit[None, None]).reshape(FILTERS, count, SOURCES)
    plain = filtered.reshape(FILTERS, count, SOURCES)
    local = jnp.einsum("kms,lmt->kslt", weighted, plain, precision=lax.Precision.HIGHEST)
    local = local.reshape(FILTERS * SOURCES, FILTERS * SOURCES)
    summed = lax.psum(local, ("gx", "gy"))
    cells = e_field.shape[1] * lax.axis_size("gx") * e_field.shape[2] * lax.axis_size("gy") * NZ
    return (e_field, h_field, summed / cells)


def solution(mesh):
    in_specs = (P(None, "gx", "gy", None), P(None, "gx", "gy", None), P("gx", "gy", None), P(), P())
    out_specs = (P(None, "gx", "gy", None), P(None, "gx", "gy", None), P())
    return jax.shard_map(body, mesh=mesh, in_specs=in_specs, out_specs=out_specs, check_vma=False)
```

profile of v0, /device:TPU:1, one launch (start us, length us, event | category | flops | bytes accessed | tf_op | source)
XLA Modules:
  0.0 369.0 jit_solution(447718432147306307)
XLA Ops:
  1.4 20.9 %collective-permute-start.1 = (f32[2,1,16,128]{3,2,1,0:T(8,128)S(1)}, f32[2,1,16,128]{3,2,1,0:T(8,128)S(1)}, u32[]{:S(2)}, u32[]{:S(2)}) collective-permute-start(f32[2,1,16,128]{3,2,1,0:T(8,128)S(1)} %slice.390), channel_id=1, source_target_pairs={{0,496},{16,0},{32,16},{48,32},{64,48},{80,64},{96,80},{112,96},{1... | collective-permute-start | bytes 49160 | tf_op jit(solution)/shard_map/ppermute | solution.py:17
  23.2 2.9 collective-permute-start
  29.6 14.0 %mul.282 = f32[24576,2]{1,0:T(8,128)} reshape(f32[3,8,16,128]{3,2,1,0:T(8,128)S(1)} %mul.281) | data formatting | bytes 393216 | tf_op jit(solution)/shard_map/mul | solution.py:77
  43.6 7.5 %copy.782 = f32[2,24576]{1,0:T(2,128)S(1)} copy(f32[2,24576]{0,1:T(8,128)} %bitcast.290) | data formatting | bytes 393216 | tf_op jit(solution)/shard_map/mul | solution.py:77
  51.5 2.7 collective-permute-start.2
  54.2 1.9 collective-permute-start.3
  57.0 14.7 %collective-permute-done.3 = f32[2,1,16,128]{3,2,1,0:T(8,128)S(1)} collective-permute-done((f32[2,1,16,128]{3,2,1,0:T(8,128)S(1)}, f32[2,1,16,128]{3,2,1,0:T(8,128)S(1)}, u32[]{:S(2)}, u32[]{:S(2)}) %collective-permute-start.3) | collective-permute-done | bytes 16416 | tf_op jit(solution)/shard_map/ppermute | solution.py:17
  71.8 1.9 collective-permute-start.5
  73.9 2.5 collective-permute-done.5
  76.4 6.3 %collective-permute-start.4 = (f32[2,8,1,128]{3,1,2,0:T(8,128)S(1)}, f32[2,8,1,128]{3,1,2,0:T(8,128)S(1)}, u32[]{:S(2)}, u32[]{:S(2)}) collective-permute-start(f32[2,8,1,128]{3,1,2,0:T(8,128)S(1)} %pad_maximum_fusion.9), channel_id=1, source_target_pairs={{0,15},{1,0},{2,1},{3,2},{4,3},{5,4},{6,5},{7,6},{8,7},{9,8},{10,9... | collective-permute-start | bytes 24584 | tf_op jit(solution)/shard_map/ppermute | solution.py:17
  82.9 14.0 %mul.260 = f32[24576,2]{1,0:T(8,128)} reshape(f32[3,8,16,128]{3,2,1,0:T(8,128)S(1)} %pad_maximum_fusion.1) | data formatting | bytes 393216 | tf_op jit(solution)/shard_map/mul | solution.py:75
  96.9 7.5 %copy.777 = f32[2,24576]{1,0:T(2,128)S(1)} copy(f32[2,24576]{0,1:T(8,128)} %bitcast.291) | data formatting | bytes 393216 | tf_op jit(solution)/shard_map/mul | solution.py:75
  104.6 1.9 collective-permute-start.6
  108.5 4.7 %collective-permute-done.6 = f32[2,8,1,128]{3,1,2,0:T(8,128)S(1)} collective-permute-done((f32[2,8,1,128]{3,1,2,0:T(8,128)S(1)}, f32[2,8,1,128]{3,1,2,0:T(8,128)S(1)}, u32[]{:S(2)}, u32[]{:S(2)}) %collective-permute-start.6) | collective-permute-done | bytes 8224 | tf_op jit(solution)/shard_map/ppermute | solution.py:17
  113.2 10.8 %collective-permute-done.7 = f32[2,1,16,128]{3,2,1,0:T(8,128)S(1)} collective-permute-done((f32[2,1,16,128]{3,2,1,0:T(8,128)S(1)}, f32[2,1,16,128]{3,2,1,0:T(8,128)S(1)}, u32[]{:S(2)}, u32[]{:S(2)}) %collective-permute-start.7) | collective-permute-done | bytes 16416 | tf_op jit(solution)/shard_map/ppermute | solution.py:17
  124.2 4.1 %collective-permute-start.9 = (f32[2,1,16,128]{3,2,1,0:T(8,128)S(1)}, f32[2,1,16,128]{3,2,1,0:T(8,128)S(1)}, u32[]{:S(2)}, u32[]{:S(2)}) collective-permute-start(f32[2,1,16,128]{3,2,1,0:T(8,128)S(1)} %pad_maximum_fusion.5), channel_id=1, source_target_pairs={{0,496},{16,0},{32,16},{48,32},{64,48},{80,64},{96,80},{112,96},{1... | collective-permute-start | bytes 49160 | tf_op jit(solution)/shard_map/ppermute | solution.py:17
  129.2 11.8 %collective-permute-start.8 = (f32[2,8,1,128]{3,1,2,0:T(8,128)S(1)}, f32[2,8,1,128]{3,1,2,0:T(8,128)S(1)}, u32[]{:S(2)}, u32[]{:S(2)}) collective-permute-start(f32[2,8,1,128]{3,1,2,0:T(8,128)S(1)} %pad_maximum_fusion.11), channel_id=1, source_target_pairs={{0,15},{1,0},{2,1},{3,2},{4,3},{5,4},{6,5},{7,6},{8,7},{9,8},{10,9... | collective-permute-start | bytes 24584 | tf_op jit(solution)/shard_map/ppermute | solution.py:17
  141.1 14.0 %mul.265 = f32[24576,2]{1,0:T(8,128)} reshape(f32[3,8,16,128]{3,2,1,0:T(8,128)S(1)} %pad_maximum_fusion.2) | data formatting | bytes 393216 | tf_op jit(solution)/shard_map/mul | solution.py:75
  155.1 7.5 %copy.778 = f32[2,24576]{1,0:T(2,128)S(1)} copy(f32[2,24576]{0,1:T(8,128)} %bitcast.292) | data formatting | bytes 393216 | tf_op jit(solution)/shard_map/mul | solution.py:75
  166.8 2.7 collective-permute-done.10
  169.5 13.3 %collective-permute-done.11 = f32[2,1,16,128]{3,2,1,0:T(8,128)S(1)} collective-permute-done((f32[2,1,16,128]{3,2,1,0:T(8,128)S(1)}, f32[2,1,16,128]{3,2,1,0:T(8,128)S(1)}, u32[]{:S(2)}, u32[]{:S(2)}) %collective-permute-start.11) | collective-permute-done | bytes 16416 | tf_op jit(solution)/shard_map/ppermute | solution.py:17
  183.0 3.4 collective-permute-start.13
  187.6 9.7 %collective-permute-start.12 = (f32[2,8,1,128]{3,1,2,0:T(8,128)S(1)}, f32[2,8,1,128]{3,1,2,0:T(8,128)S(1)}, u32[]{:S(2)}, u32[]{:S(2)}) collective-permute-start(f32[2,8,1,128]{3,1,2,0:T(8,128)S(1)} %pad_maximum_fusion.13), channel_id=1, source_target_pairs={{0,15},{1,0},{2,1},{3,2},{4,3},{5,4},{6,5},{7,6},{8,7},{9,8},{10,9... | collective-permute-start | bytes 24584 | tf_op jit(solution)/shard_map/ppermute | solution.py:17
  197.4 14.0 %mul.271 = f32[24576,2]{1,0:T(8,128)} reshape(f32[3,8,16,128]{3,2,1,0:T(8,128)S(1)} %pad_maximum_fusion.3) | data formatting | bytes 393216 | tf_op jit(solution)/shard_map/mul | solution.py:75
  211.4 7.5 %copy.779 = f32[2,24576]{1,0:T(2,128)S(1)} copy(f32[2,24576]{0,1:T(8,128)} %bitcast.293) | data formatting | bytes 393216 | tf_op jit(solution)/shard_map/mul | solution.py:75
  219.2 1.9 collective-permute-start.14
  221.2 2.1 collective-permute-start.15
  223.3 2.5 collective-permute-done.14
  225.8 13.4 %collective-permute-done.15 = f32[2,1,16,128]{3,2,1,0:T(8,128)S(1)} collective-permute-done((f32[2,1,16,128]{3,2,1,0:T(8,128)S(1)}, f32[2,1,16,128]{3,2,1,0:T(8,128)S(1)}, u32[]{:S(2)}, u32[]{:S(2)}) %collective-permute-start.15) | collective-permute-done | bytes 16416 | tf_op jit(solution)/shard_map/ppermute | solution.py:17
  239.3 14.0 %mul.277 = f32[24576,2]{1,0:T(8,128)} reshape(f32[3,8,16,128]{3,2,1,0:T(8,128)S(1)} %pad_maximum_fusion) | data formatting | bytes 393216 | tf_op jit(solution)/shard_map/mul | solution.py:75
  253.3 7.5 %copy.780 = f32[2,24576]{1,0:T(2,128)S(1)} copy(f32[2,24576]{0,1:T(8,128)} %bitcast.294) | data formatting | bytes 393216 | tf_op jit(solution)/shard_map/mul | solution.py:75
  264.8 103.5 %psum.7 = f32[8,8]{1,0:T(8,128)S(1)} all-reduce(f32[8,8]{1,0:T(8,128)S(1)} %fusion.85), channel_id=1, replica_groups=mesh['gx'=32,'gy'=16] {'gx','gy'}, use_global_device_ids=true, to_apply=%region_1.0 | all-reduce | flops 64 | bytes 512 | tf_op jit(solution)/shard_map/psum | solution.py:81
  (145 shorter events, 20.1 us)
Async XLA Ops:
  1.4 49.8 %collective-permute-start.1 = (f32[2,1,16,128]{3,2,1,0:T(8,128)S(1)}, f32[2,1,16,128]{3,2,1,0:T(8,128)S(1)}, u32[]{:S(2)}, u32[]{:S(2)}) collective-permute-start(f32[2,1,16,128]{3,2,1,0:T(8,128)S(1)} %slice.390), channel_id=1, source_target_pairs={{0,496},{16,0},{32,16},{48,32},{64,48},{80,64},{96,80},{112,96},{1... | collective-permute-start | bytes 49160 | tf_op jit(solution)/shard_map/ppermute | solution.py:17
  23.2 28.0 %collective-permute-start = (f32[2,8,1,128]{3,1,2,0:T(8,128)S(1)}, f32[2,8,1,128]{3,1,2,0:T(8,128)S(1)}, u32[]{:S(2)}, u32[]{:S(2)}) collective-permute-start(f32[2,8,1,128]{3,1,2,0:T(8,128)S(1)} %pad_maximum_fusion.7), channel_id=1, source_target_pairs={{0,15},{1,0},{2,1},{3,2},{4,3},{5,4},{6,5},{7,6},{8,7},{9,8},{10,9... | collective-permute-start | bytes 24584 | tf_op jit(solution)/shard_map/ppermute | solution.py:17
  29.6 21.6 %copy-start = (f32[3,8,16,128]{3,2,1,0:T(8,128)S(1)}, f32[3,8,16,128]{3,2,1,0:T(8,128)}, u32[]{:S(2)}) copy-start(f32[3,8,16,128]{3,2,1,0:T(8,128)} %param.5) | copy-start | bytes 589828
  29.6 21.8 %copy-start.2 = (f32[3,8,16,128]{3,2,1,0:T(8,128)S(1)}, f32[3,8,16,128]{3,2,1,0:T(8,128)}, u32[]{:S(2)}) copy-start(f32[3,8,16,128]{3,2,1,0:T(8,128)} %param.6) | copy-start | bytes 589828
  51.5 5.5 %collective-permute-start.2 = (f32[2,8,1,128]{3,1,2,0:T(8,128)S(1)}, f32[2,8,1,128]{3,1,2,0:T(8,128)S(1)}, u32[]{:S(2)}, u32[]{:S(2)}) collective-permute-start(f32[2,8,1,128]{3,1,2,0:T(8,128)S(1)} %pad_maximum_fusion.8), channel_id=1, source_target_pairs={{0,1},{1,2},{2,3},{3,4},{4,5},{5,6},{6,7},{7,8},{8,9},{9,10},{10,1... | collective-permute-start | bytes 24584 | tf_op jit(solution)/shard_map/ppermute | solution.py:17
  54.2 17.4 %collective-permute-start.3 = (f32[2,1,16,128]{3,2,1,0:T(8,128)S(1)}, f32[2,1,16,128]{3,2,1,0:T(8,128)S(1)}, u32[]{:S(2)}, u32[]{:S(2)}) collective-permute-start(f32[2,1,16,128]{3,2,1,0:T(8,128)S(1)} %slice.517), channel_id=1, source_target_pairs={{0,16},{16,32},{32,48},{48,64},{64,80},{80,96},{96,112},{112,128},... | collective-permute-start | bytes 49160 | tf_op jit(solution)/shard_map/ppermute | solution.py:17
  71.8 4.5 %collective-permute-start.5 = (f32[2,1,16,128]{3,2,1,0:T(8,128)S(1)}, f32[2,1,16,128]{3,2,1,0:T(8,128)S(1)}, u32[]{:S(2)}, u32[]{:S(2)}) collective-permute-start(f32[2,1,16,128]{3,2,1,0:T(8,128)S(1)} %pad_maximum_fusion.6), channel_id=1, source_target_pairs={{0,496},{16,0},{32,16},{48,32},{64,48},{80,64},{96,80},{112,96},{1... | collective-permute-start | bytes 49160 | tf_op jit(solution)/shard_map/ppermute | solution.py:17
  76.4 28.0 %collective-permute-start.4 = (f32[2,8,1,128]{3,1,2,0:T(8,128)S(1)}, f32[2,8,1,128]{3,1,2,0:T(8,128)S(1)}, u32[]{:S(2)}, u32[]{:S(2)}) collective-permute-start(f32[2,8,1,128]{3,1,2,0:T(8,128)S(1)} %pad_maximum_fusion.9), channel_id=1, source_target_pairs={{0,15},{1,0},{2,1},{3,2},{4,3},{5,4},{6,5},{7,6},{8,7},{9,8},{10,9... | collective-permute-start | bytes 24584 | tf_op jit(solution)/shard_map/ppermute | solution.py:17
  104.6 8.6 %collective-permute-start.6 = (f32[2,8,1,128]{3,1,2,0:T(8,128)S(1)}, f32[2,8,1,128]{3,1,2,0:T(8,128)S(1)}, u32[]{:S(2)}, u32[]{:S(2)}) collective-permute-start(f32[2,8,1,128]{3,1,2,0:T(8,128)S(1)} %pad_maximum_fusion.10), channel_id=1, source_target_pairs={{0,1},{1,2},{2,3},{3,4},{4,5},{5,6},{6,7},{7,8},{8,9},{9,10},{10,1... | collective-permute-start | bytes 24584 | tf_op jit(solution)/shard_map/ppermute | solution.py:17
  106.6 17.4 %collective-permute-start.7 = (f32[2,1,16,128]{3,2,1,0:T(8,128)S(1)}, f32[2,1,16,128]{3,2,1,0:T(8,128)S(1)}, u32[]{:S(2)}, u32[]{:S(2)}) collective-permute-start(f32[2,1,16,128]{3,2,1,0:T(8,128)S(1)} %slice.545), channel_id=1, source_target_pairs={{0,16},{16,32},{32,48},{48,64},{64,80},{80,96},{96,112},{112,128},... | collective-permute-start | bytes 49160 | tf_op jit(solution)/shard_map/ppermute | solution.py:17
  124.2 5.0 %collective-permute-start.9 = (f32[2,1,16,128]{3,2,1,0:T(8,128)S(1)}, f32[2,1,16,128]{3,2,1,0:T(8,128)S(1)}, u32[]{:S(2)}, u32[]{:S(2)}) collective-permute-start(f32[2,1,16,128]{3,2,1,0:T(8,128)S(1)} %pad_maximum_fusion.5), channel_id=1, source_target_pairs={{0,496},{16,0},{32,16},{48,32},{64,48},{80,64},{96,80},{112,96},{1... | collective-permute-start | bytes 49160 | tf_op jit(solution)/shard_map/ppermute | solution.py:17
  129.2 33.5 %collective-permute-start.8 = (f32[2,8,1,128]{3,1,2,0:T(8,128)S(1)}, f32[2,8,1,128]{3,1,2,0:T(8,128)S(1)}, u32[]{:S(2)}, u32[]{:S(2)}) collective-permute-start(f32[2,8,1,128]{3,1,2,0:T(8,128)S(1)} %pad_maximum_fusion.11), channel_id=1, source_target_pairs={{0,15},{1,0},{2,1},{3,2},{4,3},{5,4},{6,5},{7,6},{8,7},{9,8},{10,9... | collective-permute-start | bytes 24584 | tf_op jit(solution)/shard_map/ppermute | solution.py:17
  162.9 6.6 %collective-permute-start.10 = (f32[2,8,1,128]{3,1,2,0:T(8,128)S(1)}, f32[2,8,1,128]{3,1,2,0:T(8,128)S(1)}, u32[]{:S(2)}, u32[]{:S(2)}) collective-permute-start(f32[2,8,1,128]{3,1,2,0:T(8,128)S(1)} %pad_maximum_fusion.12), channel_id=1, source_target_pairs={{0,1},{1,2},{2,3},{3,4},{4,5},{5,6},{6,7},{7,8},{8,9},{9,10},{10,1... | collective-permute-start | bytes 24584 | tf_op jit(solution)/shard_map/ppermute | solution.py:17
  164.9 18.0 %collective-permute-start.11 = (f32[2,1,16,128]{3,2,1,0:T(8,128)S(1)}, f32[2,1,16,128]{3,2,1,0:T(8,128)S(1)}, u32[]{:S(2)}, u32[]{:S(2)}) collective-permute-start(f32[2,1,16,128]{3,2,1,0:T(8,128)S(1)} %slice.573), channel_id=1, source_target_pairs={{0,16},{16,32},{32,48},{48,64},{64,80},{80,96},{96,112},{112,128},... | collective-permute-start | bytes 49160 | tf_op jit(solution)/shard_map/ppermute | solution.py:17
  183.0 4.5 %collective-permute-start.13 = (f32[2,1,16,128]{3,2,1,0:T(8,128)S(1)}, f32[2,1,16,128]{3,2,1,0:T(8,128)S(1)}, u32[]{:S(2)}, u32[]{:S(2)}) collective-permute-start(f32[2,1,16,128]{3,2,1,0:T(8,128)S(1)} %pad_maximum_fusion.4), channel_id=1, source_target_pairs={{0,496},{16,0},{32,16},{48,32},{64,48},{80,64},{96,80},{112,96},{1... | collective-permute-start | bytes 49160 | tf_op jit(solution)/shard_map/ppermute | solution.py:17
  187.6 31.4 %collective-permute-start.12 = (f32[2,8,1,128]{3,1,2,0:T(8,128)S(1)}, f32[2,8,1,128]{3,1,2,0:T(8,128)S(1)}, u32[]{:S(2)}, u32[]{:S(2)}) collective-permute-start(f32[2,8,1,128]{3,1,2,0:T(8,128)S(1)} %pad_maximum_fusion.13), channel_id=1, source_target_pairs={{0,15},{1,0},{2,1},{3,2},{4,3},{5,4},{6,5},{7,6},{8,7},{9,8},{10,9... | collective-permute-start | bytes 24584 | tf_op jit(solution)/shard_map/ppermute | solution.py:17
  219.1 41.8 %copy-start.1 = (f32[3,8,16,128]{3,2,1,0:T(8,128)}, f32[3,8,16,128]{3,2,1,0:T(8,128)S(1)}, u32[]{:S(2)}) copy-start(f32[3,8,16,128]{3,2,1,0:T(8,128)S(1)} %fusion.3) | copy-start | bytes 589828
  219.2 6.6 %collective-permute-start.14 = (f32[2,8,1,128]{3,1,2,0:T(8,128)S(1)}, f32[2,8,1,128]{3,1,2,0:T(8,128)S(1)}, u32[]{:S(2)}, u32[]{:S(2)}) collective-permute-start(f32[2,8,1,128]{3,1,2,0:T(8,128)S(1)} %pad_maximum_fusion.14), channel_id=1, source_target_pairs={{0,1},{1,2},{2,3},{3,4},{4,5},{5,6},{6,7},{7,8},{8,9},{9,10},{10,1... | collective-permute-start | bytes 24584 | tf_op jit(solution)/shard_map/ppermute | solution.py:17
  221.2 18.0 %collective-permute-start.15 = (f32[2,1,16,128]{3,2,1,0:T(8,128)S(1)}, f32[2,1,16,128]{3,2,1,0:T(8,128)S(1)}, u32[]{:S(2)}, u32[]{:S(2)}) collective-permute-start(f32[2,1,16,128]{3,2,1,0:T(8,128)S(1)} %slice.602), channel_id=1, source_target_pairs={{0,16},{16,32},{32,48},{48,64},{64,80},{80,96},{96,112},{112,128},... | collective-permute-start | bytes 49160 | tf_op jit(solution)/shard_map/ppermute | solution.py:17
  239.3 21.6 %copy-start.3 = (f32[3,8,16,128]{3,2,1,0:T(8,128)}, f32[3,8,16,128]{3,2,1,0:T(8,128)S(1)}, u32[]{:S(2)}) copy-start(f32[3,8,16,128]{3,2,1,0:T(8,128)S(1)} %pad_maximum_fusion) | copy-start | bytes 589828
where the time goes:
time: 370 us; the launch traced here: 369 us
  local copies, waits for them, and re-layouts  113 us (31%)
  blocking collectives  104 us (28%)
  starting transfers between devices  77.3 us (21%)
  waiting for transfers between devices  67.1 us (18%)
  other arithmetic  4.46 us (1%)
    psum x1, blocking collectives, body(): summed = lax.psum(local, ('gx', 'gy'))  104 us
    mul x8, local copies, waits for them, and re-layouts, body(): filtered = filtered + weights[:, None, None, None, None] * e_field[None]  86.2 us
    ppermute x16, starting transfers between devices, from_behind(): return lax.ppermute(value, axis, pairs)  77.3 us
    ppermute x16, waiting for transfers between devices, from_behind(): return lax.ppermute(value, axis, pairs)  67.1 us
    mul x4, local copies, waits for them, and re-layouts, body(): weighted = (filtered * permit[None, None]).reshape(FILTERS, count, SOURCES)  22.1 us
  transfers between devices with their start and end apart: 16, of which 11 were waited for; matrix products, arithmetic and copies ran while one was open for 25% of the time, Pallas kernels for 0%

commit v1 on v0

--- a/solution.py
+++ b/solution.py
@@ -78,7 +78,7 @@
     plain = filtered.reshape(FILTERS, count, SOURCES)
     local = jnp.einsum("kms,lmt->kslt", weighted, plain, precision=lax.Precision.HIGHEST)
     local = local.reshape(FILTERS * SOURCES, FILTERS * SOURCES)
-    summed = lax.psum(local, ("gx", "gy"))
+    summed = jnp.sum(lax.all_gather(local, ("gx", "gy")), axis=0)
     cells = e_field.shape[1] * lax.axis_size("gx") * e_field.shape[2] * lax.axis_size("gy") * NZ
     return (e_field, h_field, summed / cells)
 

time: 370 us -> 1090 us (2.95)
  the two profiles are of different devices: /device:TPU:1 before, /device:TPU:3 now
where the time goes in v1:
time: 1090 us
  blocking collectives  837 us (77%)
  local copies, waits for them, and re-layouts  113 us (10%)
  starting transfers between devices  96.8 us (9%)
  waiting for transfers between devices  32 us (3%)
    all_gather x1, blocking collectives, body(): summed = jnp.sum(lax.all_gather(local, ('gx', 'gy')), axis=0)  837 us
    ppermute x16, starting transfers between devices, from_behind(): return lax.ppermute(value, axis, pairs)  96.8 us
    mul x8, local copies, waits for them, and re-layouts, body(): filtered = filtered + weights[:, None, None, None, None] * e_field[None]  86.2 us
    ppermute x16, waiting for transfers between devices, from_behind(): return lax.ppermute(value, axis, pairs)  32 us
    mul x4, local copies, waits for them, and re-layouts, body(): weighted = (filtered * permit[None, None]).reshape(FILTERS, count, SOURCES)  22.1 us
  transfers between devices with their start and end apart: 16, of which 10 were waited for; matrix products, arithmetic and copies ran while one was open for 8% of the time, Pallas kernels for 0%

profile of v1, /device:TPU:3, one launch (start us, length us, event | category | flops | bytes accessed | tf_op | source)
XLA Modules:
  0.0 1087.1 jit_solution(1790032377414696749)
XLA Ops:
  1.4 1.9 collective-permute-start.1
  4.2 8.5 collective-permute-start
  16.2 14.0 %mul.282 = f32[24576,2]{1,0:T(8,128)} reshape(f32[3,8,16,128]{3,2,1,0:T(8,128)S(1)} %mul.281) | data formatting | bytes 393216 | tf_op jit(solution)/shard_map/mul | solution.py:77
  30.2 7.5 copy.782
  38.1 1.9 collective-permute-start.2
  40.1 1.9 collective-permute-start.3
  42.0 3.7 collective-permute-done.2
  45.7 11.0 %collective-permute-done.3 = f32[2,1,16,128]{3,2,1,0:T(8,128)S(1)} collective-permute-done((f32[2,1,16,128]{3,2,1,0:T(8,128)S(1)}, f32[2,1,16,128]{3,2,1,0:T(8,128)S(1)}, u32[]{:S(2)}, u32[]{:S(2)}) %collective-permute-start.3) | collective-permute-done | bytes 16416 | tf_op jit(solution)/shard_map/ppermute | solution.py:17
  56.9 16.3 %collective-permute-start.5 = (f32[2,1,16,128]{3,2,1,0:T(8,128)S(1)}, f32[2,1,16,128]{3,2,1,0:T(8,128)S(1)}, u32[]{:S(2)}, u32[]{:S(2)}) collective-permute-start(f32[2,1,16,128]{3,2,1,0:T(8,128)S(1)} %pad_maximum_fusion.6), channel_id=1, source_target_pairs={{0,496},{16,0},{32,16},{48,32},{64,48},{80,64},{96,80},{112,96},{1... | collective-permute-start | bytes 49160 | tf_op jit(solution)/shard_map/ppermute | solution.py:17
  74.1 6.0 collective-permute-start.4
  80.3 14.0 %mul.260 = f32[24576,2]{1,0:T(8,128)} reshape(f32[3,8,16,128]{3,2,1,0:T(8,128)S(1)} %pad_maximum_fusion.1) | data formatting | bytes 393216 | tf_op jit(solution)/shard_map/mul | solution.py:75
  94.3 7.5 copy.777
  102.0 1.9 collective-permute-start.6
  104.0 1.9 collective-permute-start.7
  105.9 5.0 collective-permute-done.6
  111.2 14.4 %collective-permute-start.9 = (f32[2,1,16,128]{3,2,1,0:T(8,128)S(1)}, f32[2,1,16,128]{3,2,1,0:T(8,128)S(1)}, u32[]{:S(2)}, u32[]{:S(2)}) collective-permute-start(f32[2,1,16,128]{3,2,1,0:T(8,128)S(1)} %pad_maximum_fusion.5), channel_id=1, source_target_pairs={{0,496},{16,0},{32,16},{48,32},{64,48},{80,64},{96,80},{112,96},{1... | collective-permute-start | bytes 49160 | tf_op jit(solution)/shard_map/ppermute | solution.py:17
  126.4 10.0 collective-permute-start.8
  136.5 14.0 %mul.265 = f32[24576,2]{1,0:T(8,128)} reshape(f32[3,8,16,128]{3,2,1,0:T(8,128)S(1)} %pad_maximum_fusion.2) | data formatting | bytes 393216 | tf_op jit(solution)/shard_map/mul | solution.py:75
  150.5 7.5 copy.778
  158.3 1.9 collective-permute-start.10
  160.3 1.9 collective-permute-start.11
  162.2 5.0 collective-permute-done.10
  167.5 16.9 %collective-permute-start.13 = (f32[2,1,16,128]{3,2,1,0:T(8,128)S(1)}, f32[2,1,16,128]{3,2,1,0:T(8,128)S(1)}, u32[]{:S(2)}, u32[]{:S(2)}) collective-permute-start(f32[2,1,16,128]{3,2,1,0:T(8,128)S(1)} %pad_maximum_fusion.4), channel_id=1, source_target_pairs={{0,496},{16,0},{32,16},{48,32},{64,48},{80,64},{96,80},{112,96},{1... | collective-permute-start | bytes 49160 | tf_op jit(solution)/shard_map/ppermute | solution.py:17
  185.3 7.4 collective-permute-start.12
  192.8 14.0 %mul.271 = f32[24576,2]{1,0:T(8,128)} reshape(f32[3,8,16,128]{3,2,1,0:T(8,128)S(1)} %pad_maximum_fusion.3) | data formatting | bytes 393216 | tf_op jit(solution)/shard_map/mul | solution.py:75
  206.8 7.5 copy.779
  214.6 1.9 collective-permute-start.14
  216.6 2.1 collective-permute-start.15
  218.7 4.8 collective-permute-done.14
  223.8 14.0 %mul.277 = f32[24576,2]{1,0:T(8,128)} reshape(f32[3,8,16,128]{3,2,1,0:T(8,128)S(1)} %pad_maximum_fusion) | data formatting | bytes 393216 | tf_op jit(solution)/shard_map/mul | solution.py:75
  237.8 7.5 copy.780
  249.3 836.6 %all-gather = f32[4096,8]{1,0:T(8,128)S(1)} all-gather(f32[8,8]{1,0:T(8,128)S(1)} %fusion.85), channel_id=2, replica_groups=mesh['gx'=32,'gy'=16] {'gx','gy'}, dimensions={0}, use_global_device_ids=true | all-gather | bytes 131328 | tf_op jit(solution)/shard_map/all_gather | solution.py:81
  (146 shorter events, 14.8 us)
Async XLA Ops:
  1.4 36.4 %collective-permute-start.1 = (f32[2,1,16,128]{3,2,1,0:T(8,128)S(1)}, f32[2,1,16,128]{3,2,1,0:T(8,128)S(1)}, u32[]{:S(2)}, u32[]{:S(2)}) collective-permute-start(f32[2,1,16,128]{3,2,1,0:T(8,128)S(1)} %slice.390), channel_id=1, source_target_pairs={{0,496},{16,0},{32,16},{48,32},{64,48},{80,64},{96,80},{112,96},{1... | collective-permute-start | bytes 49160 | tf_op jit(solution)/shard_map/ppermute | solution.py:17
  4.2 33.6 %collective-permute-start = (f32[2,8,1,128]{3,1,2,0:T(8,128)S(1)}, f32[2,8,1,128]{3,1,2,0:T(8,128)S(1)}, u32[]{:S(2)}, u32[]{:S(2)}) collective-permute-start(f32[2,8,1,128]{3,1,2,0:T(8,128)S(1)} %pad_maximum_fusion.7), channel_id=1, source_target_pairs={{0,15},{1,0},{2,1},{3,2},{4,3},{5,4},{6,5},{7,6},{8,7},{9,8},{10,9... | collective-permute-start | bytes 24584 | tf_op jit(solution)/shard_map/ppermute | solution.py:17
  16.2 21.6 %copy-start = (f32[3,8,16,128]{3,2,1,0:T(8,128)S(1)}, f32[3,8,16,128]{3,2,1,0:T(8,128)}, u32[]{:S(2)}) copy-start(f32[3,8,16,128]{3,2,1,0:T(8,128)} %param.5) | copy-start | bytes 589828
  16.2 21.8 %copy-start.2 = (f32[3,8,16,128]{3,2,1,0:T(8,128)S(1)}, f32[3,8,16,128]{3,2,1,0:T(8,128)}, u32[]{:S(2)}) copy-start(f32[3,8,16,128]{3,2,1,0:T(8,128)} %param.6) | copy-start | bytes 589828
  38.1 7.6 collective-permute-start.2
  40.1 16.6 %collective-permute-start.3 = (f32[2,1,16,128]{3,2,1,0:T(8,128)S(1)}, f32[2,1,16,128]{3,2,1,0:T(8,128)S(1)}, u32[]{:S(2)}, u32[]{:S(2)}) collective-permute-start(f32[2,1,16,128]{3,2,1,0:T(8,128)S(1)} %slice.517), channel_id=1, source_target_pairs={{0,16},{16,32},{32,48},{48,64},{64,80},{80,96},{96,112},{112,128},... | collective-permute-start | bytes 49160 | tf_op jit(solution)/shard_map/ppermute | solution.py:17
  56.9 17.2 %collective-permute-start.5 = (f32[2,1,16,128]{3,2,1,0:T(8,128)S(1)}, f32[2,1,16,128]{3,2,1,0:T(8,128)S(1)}, u32[]{:S(2)}, u32[]{:S(2)}) collective-permute-start(f32[2,1,16,128]{3,2,1,0:T(8,128)S(1)} %pad_maximum_fusion.6), channel_id=1, source_target_pairs={{0,496},{16,0},{32,16},{48,32},{64,48},{80,64},{96,80},{112,96},{1... | collective-permute-start | bytes 49160 | tf_op jit(solution)/shard_map/ppermute | solution.py:17
  74.1 27.7 %collective-permute-start.4 = (f32[2,8,1,128]{3,1,2,0:T(8,128)S(1)}, f32[2,8,1,128]{3,1,2,0:T(8,128)S(1)}, u32[]{:S(2)}, u32[]{:S(2)}) collective-permute-start(f32[2,8,1,128]{3,1,2,0:T(8,128)S(1)} %pad_maximum_fusion.9), channel_id=1, source_target_pairs={{0,15},{1,0},{2,1},{3,2},{4,3},{5,4},{6,5},{7,6},{8,7},{9,8},{10,9... | collective-permute-start | bytes 24584 | tf_op jit(solution)/shard_map/ppermute | solution.py:17
  102.0 8.9 collective-permute-start.6
  104.0 7.0 collective-permute-start.7
  111.2 15.2 %collective-permute-start.9 = (f32[2,1,16,128]{3,2,1,0:T(8,128)S(1)}, f32[2,1,16,128]{3,2,1,0:T(8,128)S(1)}, u32[]{:S(2)}, u32[]{:S(2)}) collective-permute-start(f32[2,1,16,128]{3,2,1,0:T(8,128)S(1)} %pad_maximum_fusion.5), channel_id=1, source_target_pairs={{0,496},{16,0},{32,16},{48,32},{64,48},{80,64},{96,80},{112,96},{1... | collective-permute-start | bytes 49160 | tf_op jit(solution)/shard_map/ppermute | solution.py:17
  126.4 31.6 %collective-permute-start.8 = (f32[2,8,1,128]{3,1,2,0:T(8,128)S(1)}, f32[2,8,1,128]{3,1,2,0:T(8,128)S(1)}, u32[]{:S(2)}, u32[]{:S(2)}) collective-permute-start(f32[2,8,1,128]{3,1,2,0:T(8,128)S(1)} %pad_maximum_fusion.11), channel_id=1, source_target_pairs={{0,15},{1,0},{2,1},{3,2},{4,3},{5,4},{6,5},{7,6},{8,7},{9,8},{10,9... | collective-permute-start | bytes 24584 | tf_op jit(solution)/shard_map/ppermute | solution.py:17
  158.3 8.9 collective-permute-start.10
  160.3 7.1 collective-permute-start.11
  167.5 17.7 %collective-permute-start.13 = (f32[2,1,16,128]{3,2,1,0:T(8,128)S(1)}, f32[2,1,16,128]{3,2,1,0:T(8,128)S(1)}, u32[]{:S(2)}, u32[]{:S(2)}) collective-permute-start(f32[2,1,16,128]{3,2,1,0:T(8,128)S(1)} %pad_maximum_fusion.4), channel_id=1, source_target_pairs={{0,496},{16,0},{32,16},{48,32},{64,48},{80,64},{96,80},{112,96},{1... | collective-permute-start | bytes 49160 | tf_op jit(solution)/shard_map/ppermute | solution.py:17
  185.3 29.1 %collective-permute-start.12 = (f32[2,8,1,128]{3,1,2,0:T(8,128)S(1)}, f32[2,8,1,128]{3,1,2,0:T(8,128)S(1)}, u32[]{:S(2)}, u32[]{:S(2)}) collective-permute-start(f32[2,8,1,128]{3,1,2,0:T(8,128)S(1)} %pad_maximum_fusion.13), channel_id=1, source_target_pairs={{0,15},{1,0},{2,1},{3,2},{4,3},{5,4},{6,5},{7,6},{8,7},{9,8},{10,9... | collective-permute-start | bytes 24584 | tf_op jit(solution)/shard_map/ppermute | solution.py:17
  214.5 30.9 %copy-start.1 = (f32[3,8,16,128]{3,2,1,0:T(8,128)}, f32[3,8,16,128]{3,2,1,0:T(8,128)S(1)}, u32[]{:S(2)}) copy-start(f32[3,8,16,128]{3,2,1,0:T(8,128)S(1)} %fusion.3) | copy-start | bytes 589828
  214.6 8.9 collective-permute-start.14
  216.6 7.1 collective-permute-start.15
  223.8 21.6 %copy-start.3 = (f32[3,8,16,128]{3,2,1,0:T(8,128)}, f32[3,8,16,128]{3,2,1,0:T(8,128)S(1)}, u32[]{:S(2)}) copy-start(f32[3,8,16,128]{3,2,1,0:T(8,128)S(1)} %pad_maximum_fusion) | copy-start | bytes 589828
